TPU v7x, 32 devices: a whole 2x2x4 slice. The times are simulated.
32 devices in a mesh: sub: 8 (over z, y), grp: 4 (over x, core).
Axes of the slice: x: 2, y: 2, z: 4, core: 2. Of those that a mesh axis runs over, the one named last changes fastest.
Arguments:
- right_side: float32 [512, 8192], P('grp', 'sub'), may hold values from -6 to 6
- operator_block: bfloat16 [8192, 1024], P('sub'), may hold values from -0.1875 to 0.1875
- operator_diag: float32 [8192], P('sub'), may hold values from 2 to 4
- solve_block: bfloat16 [8192, 1024], P('sub'), may hold values from -0.1875 to 0.1875
- solve_diag: float32 [8192], P('sub'), may hold values from 0.5 to 1.5
- upper_rows: int32 [8, 128], P('sub'), may hold values from 0 to 1023, as said below
- lower_rows: int32 [8, 128], P('sub'), may hold values from 0 to 1023, as said below
- couple_up: bfloat16 [1024, 128], P('sub'), may hold values from -0.5 to 0.5
- couple_down: bfloat16 [1024, 128], P('sub'), may hold values from -0.5 to 0.5
- coarse_basis: bfloat16 [64, 8192], P(None, 'sub'), may hold values from -0.75 to 0.75
- coarse_inverse: bfloat16 [512, 512], P(('sub', 'grp')), may hold values from -0.046875 to 0.046875
Outputs:
- solution: float32 [512, 8192], P('grp', 'sub')
Inputs may be any that keep to these rules, and one draw needn't show every extreme that they name: `upper_rows`: local row numbers within a subdomain of 1024 unknowns; the 128 entries of one subdomain are distinct, and none of them appears in lower_rows of the same subdomain. `lower_rows`: local row numbers within a subdomain of 1024 unknowns; the 128 entries of one subdomain are distinct, and none of them appears in upper_rows of the same subdomain.
All inputs are finite; a program needn't handle non-finite values.
Results may differ from a plain program's by a relative error of at most 0.0042.
Values may be sent and summed in bfloat16 or wider, within the bound.
A program may use at most 64 MiB of HBM per device.

v0:
```python
import jax
import jax.numpy as jnp
from jax import lax
from jax.sharding import PartitionSpec as P

ITERS = 3
EPS = 1e-06


def extended(block, sides, width):
    for axis, dim in sides:
        count = lax.axis_size(axis)
        forward = [(i, i + 1) for i in range(count - 1)]
        forward.append((count - 1, 0))
        backward = [(target, source) for source, target in forward]
        low = lax.ppermute(
            lax.slice_in_dim(block, block.shape[dim] - width, None, axis=dim), axis, forward
        )
        high = lax.ppermute(lax.slice_in_dim(block, 0, width, axis=dim), axis, backward)
        block = jnp.concatenate([low, block, high], axis=dim)
    return block


def contract_last(left, right):
    return lax.dot_general(
        left, right, (((1,), (1,)), ((), ())), preferred_element_type=jnp.float32
    )


def apply_operator(
    vector, operator_block, operator_diag, upper_list, lower_list, couple_up, couple_down
):
    vector_b = vector.astype(jnp.bfloat16)
    product = contract_last(vector_b, operator_block)
    face_count = upper_list.shape[0]
    upper_face = jnp.take(vector_b, upper_list, axis=1)
    lower_face = jnp.take(vector_b, lower_list, axis=1)
    two_faces = jnp.concatenate([lower_face, upper_face], axis=1)
    padded = extended(two_faces, (("sub", 1),), face_count)
    from_below = padded[:, :face_count]
    from_above = padded[:, 3 * face_count :]
    into_upper = jnp.dot(from_above, couple_up, preferred_element_type=jnp.float32)
    into_lower = jnp.dot(from_below, couple_down, preferred_element_type=jnp.float32)
    result = operator_diag[None, :] * vector + product
    result = result.at[:, upper_list].add(into_upper)
    result = result.at[:, lower_list].add(into_lower)
    return result


def apply_solve(vector, solve_block, solve_diag, coarse_basis, coarse_inverse):
    vector_b = vector.astype(jnp.bfloat16)
    local_term = contract_last(vector_b, solve_block)
    partial_res = contract_last(coarse_basis, vector_b).astype(jnp.bfloat16)
    widened = lax.all_gather(partial_res, "grp", axis=1, tiled=True)
    solved_part = jnp.dot(
        coarse_inverse,
        lax.all_gather(widened, "sub", axis=0, tiled=True),
        preferred_element_type=jnp.float32,
    ).astype(jnp.bfloat16)
    solved = lax.all_to_all(solved_part, "grp", split_axis=1, concat_axis=0, tiled=True)
    coarse_term = lax.dot_general(
        solved, coarse_basis, (((0,), (0,)), ((), ())), preferred_element_type=jnp.float32
    )
    return solve_diag[None, :] * vector + local_term + coarse_term


def norm_of(vector):
    squares = jnp.sum(vector * vector, axis=1)
    return jnp.sqrt(lax.psum(squares, "sub") + EPS)


def least_squares(initial_norm, columns):
    extent = len(columns)
    rotations = []
    target = [initial_norm] + [jnp.zeros_like(initial_norm) for _ in range(extent)]
    triangle = []
    for j in range(extent):
        column = list(columns[j])
        for i in range(j):
            cosine, sine_value = rotations[i]
            leading = cosine * column[i] + sine_value * column[i + 1]
            column[i + 1] = -sine_value * column[i] + cosine * column[i + 1]
            column[i] = leading
        radius = jnp.sqrt(column[j] * column[j] + column[j + 1] * column[j + 1])
        cosine = column[j] / radius
        sine_value = column[j + 1] / radius
        column[j] = radius
        rotations.append((cosine, sine_value))
        target[j + 1] = -sine_value * target[j]
        target[j] = cosine * target[j]
        triangle.append(column[: j + 1])
    coeffs = [None] * extent
    for j in reversed(range(extent)):
        partial_sum = target[j]
        for k in range(j + 1, extent):
            partial_sum = partial_sum - triangle[k][j] * coeffs[k]
        coeffs[j] = partial_sum / triangle[j][j]
    return coeffs


def on_device(
    right_side,
    operator_block,
    operator_diag,
    solve_block,
    solve_diag,
    upper_rows,
    lower_rows,
    couple_up,
    couple_down,
    coarse_basis,
    coarse_inverse,
):
    upper_list = upper_rows.reshape(-1)
    lower_list = lower_rows.reshape(-1)

    def precond(vector):
        return apply_solve(vector, solve_block, solve_diag, coarse_basis, coarse_inverse)

    residual = precond(right_side)
    initial_norm = norm_of(residual)
    krylov = [residual / initial_norm[:, None]]
    columns = []
    for iteration in range(ITERS):
        candidate = precond(
            apply_operator(
                krylov[iteration],
                operator_block,
                operator_diag,
                upper_list,
                lower_list,
                couple_up,
                couple_down,
            )
        )
        heights = []
        for i in range(iteration + 1):
            height_i = lax.psum(jnp.sum(candidate * krylov[i], axis=1), "sub")
            heights.append(height_i)
            candidate = candidate - height_i[:, None] * krylov[i]
        height = norm_of(candidate)
        heights.append(height)
        krylov.append(candidate / height[:, None])
        columns.append(heights)
    coeffs = least_squares(initial_norm, columns)
    solution = coeffs[0][:, None] * krylov[0]
    for j in range(1, ITERS):
        solution = solution + coeffs[j][:, None] * krylov[j]
    return solution


def solution(mesh):
    return jax.shard_map(
        on_device,
        mesh=mesh,
        in_specs=(
            P("grp", "sub"),
            P("sub", None),
            P("sub"),
            P("sub", None),
            P("sub"),
            P("sub", None),
            P("sub", None),
            P("sub", None),
            P("sub", None),
            P(None, "sub"),
            P(("sub", "grp"), None),
        ),
        out_specs=P("grp", "sub"),
        check_vma=False,
    )
```

profile of v0, /device:TPU:0, one launch (start us, length us, event | category | flops | bytes accessed | tf_op | source)
XLA Modules:
  0.0 463.0 jit_solution(12258683345657579884)
XLA Ops:
  0.0 1.5 convolution_convert_fusion.7
  1.5 6.2 %all_gather.24 = bf16[64,512]{1,0:T(8,128)(2,1)S(1)} all-gather(bf16[64,128]{1,0:T(8,128)(2,1)S(1)} %convolution_convert_fusion.7), channel_id=1, replica_groups=mesh['sub'=8,'grp'=4] {'grp'}, dimensions={1}, use_global_device_ids=true | all-gather | bytes 81920 | tf_op jit(solution)/shard_map/all_gather | solution.py:54
  7.7 32.6 %all_gather.25 = bf16[512,512]{1,0:T(8,128)(2,1)S(1)} all-gather(bf16[64,512]{1,0:T(8,128)(2,1)S(1)} %all_gather.24), channel_id=1, replica_groups=mesh['sub'=8,'grp'=4] {'sub'}, dimensions={0}, use_global_device_ids=true | all-gather | bytes 589824 | tf_op jit(solution)/shard_map/all_gather | solution.py:57
  41.7 3.2 all-to-all-start
  50.0 2.3 convolution_add_fusion.10
  52.4 1.4 multiply_reduce_fusion.9
  53.7 21.2 %psum.70 = f32[128]{0:T(128)S(1)} all-reduce(f32[128]{0:T(128)S(1)} %get-tuple-element.18), channel_id=1, replica_groups=mesh['sub'=8,'grp'=4] {'sub'}, use_global_device_ids=true, to_apply=%region_1.0 | all-reduce | flops 128 | bytes 1024 | tf_op jit(solution)/shard_map/psum | solution.py:69
  77.0 4.7 %collective-permute-start = (bf16[128,128]{0,1:T(8,128)(2,1)S(1)}, bf16[128,128]{0,1:T(8,128)(2,1)S(1)}, u32[]{:S(2)}, u32[]{:S(2)}) collective-permute-start(bf16[128,128]{0,1:T(8,128)(2,1)S(1)} %select_bitcast_fusion.5), channel_id=1, source_target_pairs={{4,0},{8,4},{12,8},{16,12},{20,16},{24,20},{28,24},{0,28},{5,1},{9... | collective-permute-start | bytes 98312 | tf_op jit(solution)/shard_map/ppermute | solution.py:19
  81.7 3.2 convolution_add_fusion.9
  84.9 1.2 copy.54
  86.8 1.6 scatter_fusion
  88.4 1.6 scatter_fusion.1
  91.2 5.3 %all_gather.26 = bf16[64,512]{1,0:T(8,128)(2,1)S(1)} all-gather(bf16[64,128]{1,0:T(8,128)(2,1)S(1)} %fusion.1), channel_id=1, replica_groups=mesh['sub'=8,'grp'=4] {'grp'}, dimensions={1}, use_global_device_ids=true | all-gather | bytes 81920 | tf_op jit(solution)/shard_map/all_gather | solution.py:54
  96.4 31.3 %all_gather.27 = bf16[512,512]{1,0:T(8,128)(2,1)S(1)} all-gather(bf16[64,512]{1,0:T(8,128)(2,1)S(1)} %all_gather.26), channel_id=1, replica_groups=mesh['sub'=8,'grp'=4] {'sub'}, dimensions={0}, use_global_device_ids=true | all-gather | bytes 589824 | tf_op jit(solution)/shard_map/all_gather | solution.py:57
  128.5 3.2 all-to-all-start.1
  131.8 2.7 convolution_add_fusion.8
  135.6 1.4 multiply_reduce_fusion.8
  137.0 19.2 %psum.71 = f32[128]{0:T(128)S(1)} all-reduce(f32[128]{0:T(128)S(1)} %get-tuple-element.20), channel_id=1, replica_groups=mesh['sub'=8,'grp'=4] {'sub'}, use_global_device_ids=true, to_apply=%region_5.7 | all-reduce | flops 128 | bytes 1024 | tf_op jit(solution)/shard_map/psum | solution.py:138
  156.4 17.1 %psum.72 = f32[128]{0:T(128)S(1)} all-reduce(f32[128]{0:T(128)S(1)} %multiply_reduce_fusion.7), channel_id=1, replica_groups=mesh['sub'=8,'grp'=4] {'sub'}, use_global_device_ids=true, to_apply=%region_7.9 | all-reduce | flops 128 | bytes 1024 | tf_op jit(solution)/shard_map/psum | solution.py:69
  173.6 1.9 fusion.26
  176.6 1.4 gather_fusion.3
  178.1 1.4 gather_fusion.2
  181.2 2.1 collective-permute-start.3
  183.3 2.7 collective-permute-start.2
  186.0 3.2 convolution_add_fusion.7
  189.2 2.0 copy.61
  192.6 3.1 scatter_fusion.2
  195.7 3.1 scatter_fusion.3
  198.8 1.2 fusion.3
  200.0 2.0 copy.65
  202.1 5.3 %all_gather.28 = bf16[64,512]{1,0:T(8,128)(2,1)S(1)} all-gather(bf16[64,128]{1,0:T(8,128)(2,1)S(1)} %fusion.3), channel_id=1, replica_groups=mesh['sub'=8,'grp'=4] {'grp'}, dimensions={1}, use_global_device_ids=true | all-gather | bytes 81920 | tf_op jit(solution)/shard_map/all_gather | solution.py:54
  207.3 31.5 %all_gather.29 = bf16[512,512]{1,0:T(8,128)(2,1)S(1)} all-gather(bf16[64,512]{1,0:T(8,128)(2,1)S(1)} %all_gather.28), channel_id=1, replica_groups=mesh['sub'=8,'grp'=4] {'sub'}, dimensions={0}, use_global_device_ids=true | all-gather | bytes 589824 | tf_op jit(solution)/shard_map/all_gather | solution.py:57
  239.7 3.2 all-to-all-start.2
  242.9 2.8 convolution_add_fusion.6
  246.7 2.1 multiply_reduce_fusion.6
  248.8 18.0 %psum.73 = f32[128]{0:T(128)S(1)} all-reduce(f32[128]{0:T(128)S(1)} %get-tuple-element.22), channel_id=1, replica_groups=mesh['sub'=8,'grp'=4] {'sub'}, use_global_device_ids=true, to_apply=%region_11.13 | all-reduce | flops 128 | bytes 1024 | tf_op jit(solution)/shard_map/psum | solution.py:138
  266.8 1.3 multiply_reduce_fusion.5
  268.1 18.3 %psum.74 = f32[128]{0:T(128)S(1)} all-reduce(f32[128]{0:T(128)S(1)} %multiply_reduce_fusion.5), channel_id=1, replica_groups=mesh['sub'=8,'grp'=4] {'sub'}, use_global_device_ids=true, to_apply=%region_13.15 | all-reduce | flops 128 | bytes 1024 | tf_op jit(solution)/shard_map/psum | solution.py:138
  286.4 2.0 multiply_reduce_fusion.4
  288.4 18.2 %psum.75 = f32[128]{0:T(128)S(1)} all-reduce(f32[128]{0:T(128)S(1)} %get-tuple-element.14), channel_id=1, replica_groups=mesh['sub'=8,'grp'=4] {'sub'}, use_global_device_ids=true, to_apply=%region_15.17 | all-reduce | flops 128 | bytes 1024 | tf_op jit(solution)/shard_map/psum | solution.py:69
  307.1 1.8 fusion.20
  310.1 1.4 gather_fusion.5
  311.5 1.4 gather_fusion.4
  313.0 3.5 convolution_add_fusion.5
  316.6 1.2 collective-permute-start.5
  317.9 3.6 collective-permute-start.4
  321.6 2.0 copy.68
  325.0 3.1 scatter_fusion.4
  328.1 3.1 scatter_fusion.5
  331.2 1.2 fusion.5
  332.4 2.0 copy.72
  334.5 5.3 %all_gather.30 = bf16[64,512]{1,0:T(8,128)(2,1)S(1)} all-gather(bf16[64,128]{1,0:T(8,128)(2,1)S(1)} %fusion.5), channel_id=1, replica_groups=mesh['sub'=8,'grp'=4] {'grp'}, dimensions={1}, use_global_device_ids=true | all-gather | bytes 81920 | tf_op jit(solution)/shard_map/all_gather | solution.py:54
  339.7 31.5 %all_gather.31 = bf16[512,512]{1,0:T(8,128)(2,1)S(1)} all-gather(bf16[64,512]{1,0:T(8,128)(2,1)S(1)} %all_gather.30), channel_id=1, replica_groups=mesh['sub'=8,'grp'=4] {'sub'}, dimensions={0}, use_global_device_ids=true | all-gather | bytes 589824 | tf_op jit(solution)/shard_map/all_gather | solution.py:57
  372.0 3.2 all-to-all-start.3
  375.2 2.8 convolution_add_fusion.4
  379.0 2.1 multiply_reduce_fusion.3
  381.1 21.2 %psum.76 = f32[128]{0:T(128)S(1)} all-reduce(f32[128]{0:T(128)S(1)} %get-tuple-element.24), channel_id=1, replica_groups=mesh['sub'=8,'grp'=4] {'sub'}, use_global_device_ids=true, to_apply=%region_19.21 | all-reduce | flops 128 | bytes 1024 | tf_op jit(solution)/shard_map/psum | solution.py:138
  402.4 1.3 multiply_reduce_fusion.2
  403.7 17.1 %psum.77 = f32[128]{0:T(128)S(1)} all-reduce(f32[128]{0:T(128)S(1)} %multiply_reduce_fusion.2), channel_id=1, replica_groups=mesh['sub'=8,'grp'=4] {'sub'}, use_global_device_ids=true, to_apply=%region_21.23 | all-reduce | flops 128 | bytes 1024 | tf_op jit(solution)/shard_map/psum | solution.py:138
  420.8 2.2 multiply_reduce_fusion.1
  423.1 19.1 %psum.78 = f32[128]{0:T(128)S(1)} all-reduce(f32[128]{0:T(128)S(1)} %get-tuple-element.12), channel_id=1, replica_groups=mesh['sub'=8,'grp'=4] {'sub'}, use_global_device_ids=true, to_apply=%region_23.25 | all-reduce | flops 128 | bytes 1024 | tf_op jit(solution)/shard_map/psum | solution.py:138
  442.2 1.4 multiply_reduce_fusion
  443.6 17.2 %psum.79 = f32[128]{0:T(128)S(1)} all-reduce(f32[128]{0:T(128)S(1)} %multiply_reduce_fusion), channel_id=1, replica_groups=mesh['sub'=8,'grp'=4] {'sub'}, use_global_device_ids=true, to_apply=%region_25.27 | all-reduce | flops 128 | bytes 1024 | tf_op jit(solution)/shard_map/psum | solution.py:69
  460.9 2.0 multiply_add_fusion
  (141 shorter events, 23.5 us)
Async XLA Ops:
  0.0 50.0 %copy-start = (bf16[1024,1024]{1,0:T(8,128)(2,1)S(1)}, bf16[1024,1024]{1,0:T(8,128)(2,1)}, u32[]{:S(2)}) copy-start(bf16[1024,1024]{1,0:T(8,128)(2,1)} %param.16) | copy-start | bytes 6291460
  0.0 50.0 %copy-start.2 = (f32[128,1024]{1,0:T(8,128)S(1)}, f32[128,1024]{1,0:T(8,128)}, u32[]{:S(2)}) copy-start(f32[128,1024]{1,0:T(8,128)} %param.13) | copy-start | bytes 1572868
  7.7 44.7 %copy-start.1 = (bf16[64,1024]{1,0:T(8,128)(2,1)S(1)}, bf16[64,1024]{1,0:T(8,128)(2,1)}, u32[]{:S(2)}) copy-start(bf16[64,1024]{1,0:T(8,128)(2,1)} %param.22) | copy-start | bytes 393220
  41.7 10.6 %all-to-all-start = ((bf16[16,4,128]{2,0,1:T(8,128)(2,1)}), bf16[16,4,128]{2,0,1:T(8,128)(2,1)S(1)}, u32[]{:S(2)}, u32[]{:S(2)}) async-start(bf16[16,4,128]{2,0,1:T(8,128)(2,1)} %bitcast.121), calls=%async_computation | async-start | bytes 32768 | tf_op jit(solution)/shard_map/all_to_all | solution.py:60
  45.6 31.0 %copy-start.30 = (pred[128]{0:T(512)(128)(4,1)}, pred[128]{0:T(512)(128)(4,1)S(1)}, u32[]{:S(2)}) copy-start(pred[128]{0:T(512)(128)(4,1)S(1)} %compare_and_fusion) | copy-start | bytes 388
  47.5 29.4 %copy-start.28 = (pred[128]{0:T(512)(128)(4,1)}, pred[128]{0:T(512)(128)(4,1)S(1)}, u32[]{:S(2)}) copy-start(pred[128]{0:T(512)(128)(4,1)S(1)} %compare_and_fusion.1) | copy-start | bytes 388
  50.0 25.9 %copy-start.24 = (s32[1024]{0:T(1024)}, s32[1024]{0:T(1024)S(1)}, u32[]{:S(2)}) copy-start(s32[1024]{0:T(1024)S(1)} %pad_clamp_fusion.1) | copy-start | bytes 12292
  52.3 29.4 %copy-start.32 = (f32[1024]{0:T(1024)S(1)}, f32[1024]{0:T(1024)}, u32[]{:S(2)}) copy-start(f32[1024]{0:T(1024)} %param.15) | copy-start | bytes 12292
  52.3 24.5 %copy-start.25 = (s32[1024]{0:T(1024)}, s32[1024]{0:T(1024)S(1)}, u32[]{:S(2)}) copy-start(s32[1024]{0:T(1024)S(1)} %pad_clamp_fusion) | copy-start | bytes 12292
  74.9 1.9 copy-start.37
  74.9 10.0 %copy-start.16 = (f32[128]{0:T(128)}, f32[128]{0:T(128)S(1)}, u32[]{:S(2)}) copy-start(f32[128]{0:T(128)S(1)} %add_sqrt_fusion.4) | copy-start | bytes 1540
  76.8 9.4 %collective-permute-start.1 = (bf16[128,128]{0,1:T(8,128)(2,1)S(1)}, bf16[128,128]{0,1:T(8,128)(2,1)S(1)}, u32[]{:S(2)}, u32[]{:S(2)}) collective-permute-start(bf16[128,128]{0,1:T(8,128)(2,1)S(1)} %select_bitcast_fusion.4), channel_id=1, source_target_pairs={{0,4},{4,8},{8,12},{12,16},{16,20},{20,24},{24,28},{28,0},{1,5},{5... | collective-permute-start | bytes 98312 | tf_op jit(solution)/shard_map/ppermute | solution.py:16
  76.9 9.2 %copy-start.4 = (bf16[128,128]{1,0:T(8,128)(2,1)S(1)}, bf16[128,128]{1,0:T(8,128)(2,1)}, u32[]{:S(2)}) copy-start(bf16[128,128]{1,0:T(8,128)(2,1)} %param.21) | copy-start | bytes 98308
  77.0 9.5 %copy-start.7 = (bf16[128,128]{1,0:T(8,128)(2,1)S(1)}, bf16[128,128]{1,0:T(8,128)(2,1)}, u32[]{:S(2)}) copy-start(bf16[128,128]{1,0:T(8,128)(2,1)} %param.20) | copy-start | bytes 98308
  77.0 9.5 %collective-permute-start = (bf16[128,128]{0,1:T(8,128)(2,1)S(1)}, bf16[128,128]{0,1:T(8,128)(2,1)S(1)}, u32[]{:S(2)}, u32[]{:S(2)}) collective-permute-start(bf16[128,128]{0,1:T(8,128)(2,1)S(1)} %select_bitcast_fusion.5), channel_id=1, source_target_pairs={{4,0},{8,4},{12,8},{16,12},{20,16},{24,20},{28,24},{0,28},{5,1},{9... | collective-permute-start | bytes 98312 | tf_op jit(solution)/shard_map/ppermute | solution.py:19
  86.8 40.9 %copy-start.10 = (bf16[16,512]{1,0:T(8,128)(2,1)S(1)}, bf16[16,512]{1,0:T(8,128)(2,1)}, u32[]{:S(2)}) copy-start(bf16[16,512]{1,0:T(8,128)(2,1)} %param.23) | copy-start | bytes 49156
  88.4 43.4 %copy-start.13 = (f32[1024]{0:T(1024)S(1)}, f32[1024]{0:T(1024)}, u32[]{:S(2)}) copy-start(f32[1024]{0:T(1024)} %param.17) | copy-start | bytes 12292
  127.7 7.9 %copy-start.17 = (f32[128]{0:T(128)S(1)}, f32[128]{0:T(128)}, u32[]{:S(2)}) copy-start(f32[128]{0:T(128)} %copy-done.16) | copy-start | bytes 1540
  128.5 7.1 %all-to-all-start.1 = ((bf16[16,4,128]{2,0,1:T(8,128)(2,1)}), bf16[16,4,128]{2,0,1:T(8,128)(2,1)S(1)}, u32[]{:S(2)}, u32[]{:S(2)}) async-start(bf16[16,4,128]{2,0,1:T(8,128)(2,1)} %bitcast.120), calls=%async_computation.1 | async-start | bytes 32768 | tf_op jit(solution)/shard_map/all_to_all | solution.py:60
  137.0 36.6 %copy-start.3 = (f32[128,1024]{1,0:T(8,128)}, f32[128,1024]{1,0:T(8,128)S(1)}, u32[]{:S(2)}) copy-start(f32[128,1024]{1,0:T(8,128)S(1)} %get-tuple-element.21) | copy-start | bytes 1572868
  156.2 19.3 %copy-start.20 = (f32[128]{0:T(128)}, f32[128]{0:T(128)S(1)}, u32[]{:S(2)}) copy-start(f32[128]{0:T(128)S(1)} %psum.71) | copy-start | bytes 1540
  173.6 1.9 copy-start.35
  181.2 10.0 %collective-permute-start.3 = (bf16[128,128]{0,1:T(8,128)(2,1)S(1)}, bf16[128,128]{0,1:T(8,128)(2,1)S(1)}, u32[]{:S(2)}, u32[]{:S(2)}) collective-permute-start(bf16[128,128]{0,1:T(8,128)(2,1)S(1)} %select_bitcast_fusion.2), channel_id=1, source_target_pairs={{0,4},{4,8},{8,12},{12,16},{16,20},{20,24},{24,28},{28,0},{1,5},{5... | collective-permute-start | bytes 98312 | tf_op jit(solution)/shard_map/ppermute | solution.py:16
  183.3 8.3 %collective-permute-start.2 = (bf16[128,128]{0,1:T(8,128)(2,1)S(1)}, bf16[128,128]{0,1:T(8,128)(2,1)}, u32[]{:S(2)}, u32[]{:S(2)}) collective-permute-start(bf16[128,128]{0,1:T(8,128)(2,1)S(1)} %select_bitcast_fusion.3), channel_id=1, source_target_pairs={{4,0},{8,4},{12,8},{16,12},{20,16},{24,20},{28,24},{0,28},{5,1},{9... | collective-permute-start | bytes 98312 | tf_op jit(solution)/shard_map/ppermute | solution.py:19
  186.0 5.3 %copy-start.5 = (bf16[128,128]{1,0:T(8,128)(2,1)S(1)}, bf16[128,128]{1,0:T(8,128)(2,1)}, u32[]{:S(2)}) copy-start(bf16[128,128]{1,0:T(8,128)(2,1)} %param.21) | copy-start | bytes 98308
  186.0 5.6 %copy-start.8 = (bf16[128,128]{1,0:T(8,128)(2,1)S(1)}, bf16[128,128]{1,0:T(8,128)(2,1)}, u32[]{:S(2)}) copy-start(bf16[128,128]{1,0:T(8,128)(2,1)} %param.20) | copy-start | bytes 98308
  195.7 47.2 %copy-start.14 = (f32[1024]{0:T(1024)S(1)}, f32[1024]{0:T(1024)}, u32[]{:S(2)}) copy-start(f32[1024]{0:T(1024)} %param.17) | copy-start | bytes 12292
  238.9 7.9 %copy-start.18 = (f32[128]{0:T(128)S(1)}, f32[128]{0:T(128)}, u32[]{:S(2)}) copy-start(f32[128]{0:T(128)} %copy-done.16) | copy-start | bytes 1540
  239.7 7.1 %all-to-all-start.2 = ((bf16[16,4,128]{2,0,1:T(8,128)(2,1)}), bf16[16,4,128]{2,0,1:T(8,128)(2,1)S(1)}, u32[]{:S(2)}, u32[]{:S(2)}) async-start(bf16[16,4,128]{2,0,1:T(8,128)(2,1)} %bitcast.119), calls=%async_computation.2 | async-start | bytes 32768 | tf_op jit(solution)/shard_map/all_to_all | solution.py:60
  266.8 39.8 %copy-start.26 = (f32[128]{0:T(128)}, f32[128]{0:T(128)S(1)}, u32[]{:S(2)}) copy-start(f32[128]{0:T(128)S(1)} %psum.73) | copy-start | bytes 1540
  286.3 20.2 %copy-start.33 = (f32[128]{0:T(128)}, f32[128]{0:T(128)S(1)}, u32[]{:S(2)}) copy-start(f32[128]{0:T(128)S(1)} %psum.74) | copy-start | bytes 1540
  306.5 0.5 copy-start.39
  306.5 0.6 copy-start.22
  313.0 3.6 copy-start.12
  313.0 3.6 copy-start.31
  313.0 4.9 %copy-start.11 = (bf16[128,128]{1,0:T(8,128)(2,1)S(1)}, bf16[128,128]{1,0:T(8,128)(2,1)}, u32[]{:S(2)}) copy-start(bf16[128,128]{1,0:T(8,128)(2,1)} %gather_fusion.4) | copy-start | bytes 98308
  313.0 4.9 %copy-start.29 = (pred[128]{0:T(512)(128)(4,1)S(1)}, pred[128]{0:T(512)(128)(4,1)}, u32[]{:S(2)}) copy-start(pred[128]{0:T(512)(128)(4,1)} %copy-done.28) | copy-start | bytes 388
  313.0 10.6 %copy-start.6 = (bf16[128,128]{1,0:T(8,128)(2,1)S(1)}, bf16[128,128]{1,0:T(8,128)(2,1)}, u32[]{:S(2)}) copy-start(bf16[128,128]{1,0:T(8,128)(2,1)} %param.21) | copy-start | bytes 98308
  313.0 10.9 %copy-start.9 = (bf16[128,128]{1,0:T(8,128)(2,1)S(1)}, bf16[128,128]{1,0:T(8,128)(2,1)}, u32[]{:S(2)}) copy-start(bf16[128,128]{1,0:T(8,128)(2,1)} %param.20) | copy-start | bytes 98308
  316.6 7.0 %collective-permute-start.5 = (bf16[128,128]{0,1:T(8,128)(2,1)S(1)}, bf16[128,128]{0,1:T(8,128)(2,1)S(1)}, u32[]{:S(2)}, u32[]{:S(2)}) collective-permute-start(bf16[128,128]{0,1:T(8,128)(2,1)S(1)} %select_bitcast_fusion), channel_id=1, source_target_pairs={{0,4},{4,8},{8,12},{12,16},{16,20},{20,24},{24,28},{28,0},{1,5},{5... | collective-permute-start | bytes 98312 | tf_op jit(solution)/shard_map/ppermute | solution.py:16
  317.9 6.0 %collective-permute-start.4 = (bf16[128,128]{0,1:T(8,128)(2,1)S(1)}, bf16[128,128]{0,1:T(8,128)(2,1)}, u32[]{:S(2)}, u32[]{:S(2)}) collective-permute-start(bf16[128,128]{0,1:T(8,128)(2,1)S(1)} %select_bitcast_fusion.1), channel_id=1, source_target_pairs={{4,0},{8,4},{12,8},{16,12},{20,16},{24,20},{28,24},{0,28},{5,1},{9... | collective-permute-start | bytes 98312 | tf_op jit(solution)/shard_map/ppermute | solution.py:19
  328.1 47.1 %copy-start.15 = (f32[1024]{0:T(1024)S(1)}, f32[1024]{0:T(1024)}, u32[]{:S(2)}) copy-start(f32[1024]{0:T(1024)} %param.17) | copy-start | bytes 12292
  371.2 7.9 %copy-start.19 = (f32[128]{0:T(128)S(1)}, f32[128]{0:T(128)}, u32[]{:S(2)}) copy-start(f32[128]{0:T(128)} %copy-done.16) | copy-start | bytes 1540
  372.0 7.1 %all-to-all-start.3 = ((bf16[16,4,128]{2,0,1:T(8,128)(2,1)}), bf16[16,4,128]{2,0,1:T(8,128)(2,1)S(1)}, u32[]{:S(2)}, u32[]{:S(2)}) async-start(bf16[16,4,128]{2,0,1:T(8,128)(2,1)} %bitcast.118), calls=%async_computation.3 | async-start | bytes 32768 | tf_op jit(solution)/shard_map/all_to_all | solution.py:60
  378.0 42.8 %copy-start.23 = (f32[128]{0:T(128)S(1)}, f32[128]{0:T(128)}, u32[]{:S(2)}) copy-start(f32[128]{0:T(128)} %copy-done.22) | copy-start | bytes 1540
  402.4 20.7 %copy-start.21 = (f32[128]{0:T(128)S(1)}, f32[128]{0:T(128)}, u32[]{:S(2)}) copy-start(f32[128]{0:T(128)} %copy-done.20) | copy-start | bytes 1540
  402.4 20.7 %copy-start.36 = (f32[128]{0:T(128)S(1)}, f32[128]{0:T(128)}, u32[]{:S(2)}) copy-start(f32[128]{0:T(128)} %copy-done.35) | copy-start | bytes 1540
  403.6 57.2 %copy-start.27 = (f32[128]{0:T(128)S(1)}, f32[128]{0:T(128)}, u32[]{:S(2)}) copy-start(f32[128]{0:T(128)} %copy-done.26) | copy-start | bytes 1540
  403.7 57.2 %copy-start.34 = (f32[128]{0:T(128)S(1)}, f32[128]{0:T(128)}, u32[]{:S(2)}) copy-start(f32[128]{0:T(128)} %copy-done.33) | copy-start | bytes 1540
  403.7 57.2 %copy-start.38 = (f32[128]{0:T(128)S(1)}, f32[128]{0:T(128)}, u32[]{:S(2)}) copy-start(f32[128]{0:T(128)} %copy-done.37) | copy-start | bytes 1540
  403.7 57.2 %copy-start.40 = (f32[128]{0:T(128)S(1)}, f32[128]{0:T(128)}, u32[]{:S(2)}) copy-start(f32[128]{0:T(128)} %copy-done.39) | copy-start | bytes 1540
where the time goes:
time: 465 us; the launch traced here: 463 us
  blocking collectives  335 us (72%)
  other arithmetic  37.1 us (8%)
  matrix products  35.6 us (8%)
  starting transfers between devices  27.4 us (6%)
  local copies, waits for them, and re-layouts  23.7 us (5%)
    all_gather x4, blocking collectives, apply_solve(): lax.all_gather(widened, 'sub', axis=0, tiled=True)  127 us
    psum x6, blocking collectives, on_device(): height_i = lax.psum(jnp.sum(candidate * krylov[i], axis=1), 'sub')  113 us
    psum x4, blocking collectives, norm_of(): return jnp.sqrt(lax.psum(squares, 'sub') + EPS)  73.7 us
    dot_general x11, matrix products, contract_last(): lax.dot_general(left, right, (((1,), (1,)), ((), ())), preferred_element_...  24.7 us
    all_gather x4, blocking collectives, apply_solve(): widened = lax.all_gather(partial_res, 'grp', axis=1, tiled=True)  21.9 us
    all_to_all x4, starting transfers between devices, apply_solve(): lax.all_to_all(solved_part, 'grp', split_axis=1, concat_axis=0, tiled=True)  13 us
    ppermute x3, starting transfers between devices, extended(): lax.ppermute(lax.slice_in_dim(block, 0, width, axis=dim), axis, backward)  11.1 us
  transfers between devices with their start and end apart: 10, of which 3 were waited for; matrix products, arithmetic and copies ran while one was open for 6% of the time, Pallas kernels for 0%

commit v1 on v0

--- a/solution.py
+++ b/solution.py
@@ -1,3 +1,4 @@
+import functools
 import jax
 import jax.numpy as jnp
 from jax import lax
@@ -5,6 +6,23 @@
 
 ITERS = 3
 EPS = 1e-06
+
+
+def manage_side_up(z_in, mesh_name):
+    n_blocks = lax.axis_size(mesh_name)
+    part_now = sorted(((dev_j, (dev_j + 1) % n_blocks) for dev_j in range(n_blocks)))
+    back = z_in
+    rows = [back]
+    for at in range(1, n_blocks):
+        back = lax.ppermute(back, mesh_name, part_now)
+        rows.insert(0, back)
+    z_new = jnp.concatenate(rows, 1)
+    plain = lax.axis_index(mesh_name)
+    main = plain + 1
+    return jnp.roll(z_new, main * z_in.shape[1], 1)
+
+
+keep_up_flows = functools.partial(manage_side_up, mesh_name="grp")
 
 
 def extended(block, sides, width):
@@ -51,7 +69,7 @@
     vector_b = vector.astype(jnp.bfloat16)
     local_term = contract_last(vector_b, solve_block)
     partial_res = contract_last(coarse_basis, vector_b).astype(jnp.bfloat16)
-    widened = lax.all_gather(partial_res, "grp", axis=1, tiled=True)
+    widened = keep_up_flows(partial_res)
     solved_part = jnp.dot(
         coarse_inverse,
         lax.all_gather(widened, "sub", axis=0, tiled=True),

time: 465 us -> 473 us (1.017)
  waiting for transfers between devices: 3.16 us -> 34 us
  blocking collectives: 335 us -> 314 us
    ppermute x0 -> x12, waiting for transfers between devices: none -> 27.1 us  [manage_side_up(): back = lax.ppermute(back, mesh_name, part_now)]
    all_gather x4 -> x0, blocking collectives: 21.9 us -> none  [apply_solve(): widened = lax.all_gather(partial_res, 'grp', axis=1, tiled=True)]
  transfers between devices with their start and end apart: 10 -> 22, of which waited for: 3 -> 16; matrix products, arithmetic and copies ran while one was open for 6% -> 6% of each run, Pallas kernels for 0% -> 0%
where the time goes in v1:
time: 473 us; the launch traced here: 471 us
  blocking collectives  314 us (66%)
  matrix products  34.5 us (7%)
  waiting for transfers between devices  34 us (7%)
  other arithmetic  33.7 us (7%)
  starting transfers between devices  30.5 us (6%)
  local copies, waits for them, and re-layouts  23.7 us (5%)
    all_gather x4, blocking collectives, apply_solve(): lax.all_gather(widened, 'sub', axis=0, tiled=True)  127 us
    psum x6, blocking collectives, on_device(): height_i = lax.psum(jnp.sum(candidate * krylov[i], axis=1), 'sub')  113 us
    psum x4, blocking collectives, norm_of(): return jnp.sqrt(lax.psum(squares, 'sub') + EPS)  73.7 us
    ppermute x12, waiting for transfers between devices, manage_side_up(): back = lax.ppermute(back, mesh_name, part_now)  27.1 us
    dot_general x11, matrix products, contract_last(): lax.dot_general(left, right, (((1,), (1,)), ((), ())), preferred_element_...  24.5 us
    all_to_all x4, starting transfers between devices, apply_solve(): lax.all_to_all(solved_part, 'grp', split_axis=1, concat_axis=0, tiled=True)  13 us
    ppermute x3, starting transfers between devices, extended(): lax.ppermute(lax.slice_in_dim(block, 0, width, axis=dim), axis, backward)  11.2 us
  transfers between devices with their start and end apart: 22, of which 16 were waited for; matrix products, arithmetic and copies ran while one was open for 6% of the time, Pallas kernels for 0%

profile of v1, /device:TPU:0, one launch (start us, length us, event | category | flops | bytes accessed | tf_op | source)
XLA Modules:
  0.0 471.2 jit_solution(17508191079691785960)
XLA Ops:
  0.0 1.5 convolution_convert_fusion.7
  2.7 2.1 convolution_add_fusion.10
  5.3 2.2 collective-permute-start.1
  8.7 2.9 collective-permute-done.2
  11.8 32.6 %all_gather.12 = bf16[512,512]{1,0:T(8,128)(2,1)S(1)} all-gather(bf16[64,512]{1,0:T(8,128)(2,1)S(1)} %fusion.39), channel_id=1, replica_groups=mesh['sub'=8,'grp'=4] {'sub'}, dimensions={0}, use_global_device_ids=true | all-gather | bytes 589824 | tf_op jit(solution)/shard_map/all_gather | solution.py:75
  45.2 3.3 all-to-all-start
  48.5 3.8 all-to-all-done
  52.6 21.2 %psum.70 = f32[128]{0:T(128)S(1)} all-reduce(f32[128]{0:T(128)S(1)} %get-tuple-element.19), channel_id=1, replica_groups=mesh['sub'=8,'grp'=4] {'sub'}, use_global_device_ids=true, to_apply=%region_1.3 | all-reduce | flops 128 | bytes 1024 | tf_op jit(solution)/shard_map/psum | solution.py:87
  75.8 4.8 %collective-permute-start.3 = (bf16[128,128]{0,1:T(8,128)(2,1)S(1)}, bf16[128,128]{0,1:T(8,128)(2,1)}, u32[]{:S(2)}, u32[]{:S(2)}) collective-permute-start(bf16[128,128]{0,1:T(8,128)(2,1)S(1)} %select_bitcast_fusion.5), channel_id=1, source_target_pairs={{4,0},{8,4},{12,8},{16,12},{20,16},{24,20},{28,24},{0,28},{5,1},{9... | collective-permute-start | bytes 98312 | tf_op jit(solution)/shard_map/ppermute | solution.py:37
  80.5 3.2 convolution_add_fusion.9
  86.4 1.6 scatter_fusion
  88.0 1.6 scatter_fusion.1
  89.8 3.2 collective-permute-done.5
  93.0 3.2 collective-permute-done.6
  97.1 2.2 collective-permute-done.7
  99.4 31.3 %all_gather.13 = bf16[512,512]{1,0:T(8,128)(2,1)S(1)} all-gather(bf16[64,512]{1,0:T(8,128)(2,1)S(1)} %fusion.32), channel_id=1, replica_groups=mesh['sub'=8,'grp'=4] {'sub'}, dimensions={0}, use_global_device_ids=true | all-gather | bytes 589824 | tf_op jit(solution)/shard_map/all_gather | solution.py:75
  131.5 3.2 all-to-all-start.1
  134.7 2.7 convolution_add_fusion.8
  138.5 1.4 multiply_reduce_fusion.8
  139.9 19.4 %psum.71 = f32[128]{0:T(128)S(1)} all-reduce(f32[128]{0:T(128)S(1)} %get-tuple-element.21), channel_id=1, replica_groups=mesh['sub'=8,'grp'=4] {'sub'}, use_global_device_ids=true, to_apply=%region_5.8 | all-reduce | flops 128 | bytes 1024 | tf_op jit(solution)/shard_map/psum | solution.py:156
  159.6 17.1 %psum.72 = f32[128]{0:T(128)S(1)} all-reduce(f32[128]{0:T(128)S(1)} %multiply_reduce_fusion.7), channel_id=1, replica_groups=mesh['sub'=8,'grp'=4] {'sub'}, use_global_device_ids=true, to_apply=%region_7.10 | all-reduce | flops 128 | bytes 1024 | tf_op jit(solution)/shard_map/psum | solution.py:87
  176.7 1.9 fusion.54
  179.7 1.4 gather_fusion.3
  181.2 1.4 gather_fusion.2
  184.3 2.1 collective-permute-start.9
  186.4 2.7 collective-permute-start.8
  189.1 3.2 convolution_add_fusion.7
  192.3 2.0 copy.39
  195.7 3.1 scatter_fusion.2
  198.8 3.1 scatter_fusion.3
  203.2 3.2 collective-permute-done.10
  206.3 3.2 collective-permute-done.11
  209.5 2.0 copy.43
  212.8 31.7 %all_gather.14 = bf16[512,512]{1,0:T(8,128)(2,1)S(1)} all-gather(bf16[64,512]{1,0:T(8,128)(2,1)S(1)} %fusion.25), channel_id=1, replica_groups=mesh['sub'=8,'grp'=4] {'sub'}, dimensions={0}, use_global_device_ids=true | all-gather | bytes 589824 | tf_op jit(solution)/shard_map/all_gather | solution.py:75
  245.3 3.2 all-to-all-start.2
  248.5 2.8 convolution_add_fusion.6
  252.3 2.1 multiply_reduce_fusion.6
  254.4 18.0 %psum.73 = f32[128]{0:T(128)S(1)} all-reduce(f32[128]{0:T(128)S(1)} %get-tuple-element.23), channel_id=1, replica_groups=mesh['sub'=8,'grp'=4] {'sub'}, use_global_device_ids=true, to_apply=%region_11.14 | all-reduce | flops 128 | bytes 1024 | tf_op jit(solution)/shard_map/psum | solution.py:156
  273.7 18.2 %psum.74 = f32[128]{0:T(128)S(1)} all-reduce(f32[128]{0:T(128)S(1)} %multiply_reduce_fusion.5), channel_id=1, replica_groups=mesh['sub'=8,'grp'=4] {'sub'}, use_global_device_ids=true, to_apply=%region_13.16 | all-reduce | flops 128 | bytes 1024 | tf_op jit(solution)/shard_map/psum | solution.py:156
  292.0 2.0 multiply_reduce_fusion.4
  294.0 18.2 %psum.75 = f32[128]{0:T(128)S(1)} all-reduce(f32[128]{0:T(128)S(1)} %get-tuple-element.15), channel_id=1, replica_groups=mesh['sub'=8,'grp'=4] {'sub'}, use_global_device_ids=true, to_apply=%region_15.18 | all-reduce | flops 128 | bytes 1024 | tf_op jit(solution)/shard_map/psum | solution.py:87
  312.8 1.8 fusion.48
  315.8 1.4 gather_fusion.5
  317.2 1.4 gather_fusion.4
  318.7 3.5 convolution_add_fusion.5
  323.5 3.7 collective-permute-start.13
  327.3 2.0 copy.46
  330.6 3.1 scatter_fusion.4
  333.7 3.1 scatter_fusion.5
  338.1 3.2 collective-permute-done.15
  341.3 3.2 collective-permute-done.16
  344.5 2.0 copy.50
  347.7 31.4 %all_gather.15 = bf16[512,512]{1,0:T(8,128)(2,1)S(1)} all-gather(bf16[64,512]{1,0:T(8,128)(2,1)S(1)} %fusion.18), channel_id=1, replica_groups=mesh['sub'=8,'grp'=4] {'sub'}, dimensions={0}, use_global_device_ids=true | all-gather | bytes 589824 | tf_op jit(solution)/shard_map/all_gather | solution.py:75
  380.0 3.2 all-to-all-start.3
  383.2 2.8 convolution_add_fusion.4
  387.0 2.1 multiply_reduce_fusion.3
  389.1 21.4 %psum.76 = f32[128]{0:T(128)S(1)} all-reduce(f32[128]{0:T(128)S(1)} %get-tuple-element.25), channel_id=1, replica_groups=mesh['sub'=8,'grp'=4] {'sub'}, use_global_device_ids=true, to_apply=%region_19.22 | all-reduce | flops 128 | bytes 1024 | tf_op jit(solution)/shard_map/psum | solution.py:156
  410.6 1.3 multiply_reduce_fusion.2
  411.9 17.1 %psum.77 = f32[128]{0:T(128)S(1)} all-reduce(f32[128]{0:T(128)S(1)} %multiply_reduce_fusion.2), channel_id=1, replica_groups=mesh['sub'=8,'grp'=4] {'sub'}, use_global_device_ids=true, to_apply=%region_21.24 | all-reduce | flops 128 | bytes 1024 | tf_op jit(solution)/shard_map/psum | solution.py:156
  429.0 2.2 multiply_reduce_fusion.1
  431.3 19.1 %psum.78 = f32[128]{0:T(128)S(1)} all-reduce(f32[128]{0:T(128)S(1)} %get-tuple-element.13), channel_id=1, replica_groups=mesh['sub'=8,'grp'=4] {'sub'}, use_global_device_ids=true, to_apply=%region_23.26 | all-reduce | flops 128 | bytes 1024 | tf_op jit(solution)/shard_map/psum | solution.py:156
  450.4 1.4 multiply_reduce_fusion
  451.8 17.2 %psum.79 = f32[128]{0:T(128)S(1)} all-reduce(f32[128]{0:T(128)S(1)} %multiply_reduce_fusion), channel_id=1, replica_groups=mesh['sub'=8,'grp'=4] {'sub'}, use_global_device_ids=true, to_apply=%region_25.28 | all-reduce | flops 128 | bytes 1024 | tf_op jit(solution)/shard_map/psum | solution.py:87
  469.1 2.0 multiply_add_fusion
  (164 shorter events, 30.5 us)
Async XLA Ops:
  0.0 2.7 copy-start
  0.0 4.9 %copy-start.32 = (s32[1,128]{1,0:T(1,128)S(1)}, s32[1,128]{1,0:T(1,128)}, u32[]{:S(2)}) copy-start(s32[1,128]{1,0:T(1,128)} %param.21) | copy-start | bytes 1540
  0.0 4.9 %copy-start.31 = (s32[1,128]{1,0:T(1,128)S(1)}, s32[1,128]{1,0:T(1,128)}, u32[]{:S(2)}) copy-start(s32[1,128]{1,0:T(1,128)} %param.20) | copy-start | bytes 1540
  1.5 42.9 %copy-start.9 = (bf16[16,512]{1,0:T(8,128)(2,1)S(1)}, bf16[16,512]{1,0:T(8,128)(2,1)}, u32[]{:S(2)}) copy-start(bf16[16,512]{1,0:T(8,128)(2,1)} %param.25) | copy-start | bytes 49156
  1.5 3.9 collective-permute-start
  2.7 72.8 %copy-start.21 = (pred[128]{0:T(512)(128)(4,1)}, pred[128]{0:T(512)(128)(4,1)S(1)}, u32[]{:S(2)}) copy-start(pred[128]{0:T(512)(128)(4,1)S(1)} %get-tuple-element.29) | copy-start | bytes 388
  2.7 73.0 %copy-start.19 = (pred[128]{0:T(512)(128)(4,1)}, pred[128]{0:T(512)(128)(4,1)S(1)}, u32[]{:S(2)}) copy-start(pred[128]{0:T(512)(128)(4,1)S(1)} %get-tuple-element.30) | copy-start | bytes 388
  2.7 49.6 %copy-start.1 = (bf16[64,1024]{1,0:T(8,128)(2,1)S(1)}, bf16[64,1024]{1,0:T(8,128)(2,1)}, u32[]{:S(2)}) copy-start(bf16[64,1024]{1,0:T(8,128)(2,1)} %param.24) | copy-start | bytes 393220
  5.3 3.2 collective-permute-start.1
  8.5 3.2 collective-permute-start.2
  8.7 66.0 %copy-start.27 = (s32[1024]{0:T(1024)}, s32[1024]{0:T(1024)S(1)}, u32[]{:S(2)}) copy-start(s32[1024]{0:T(1024)S(1)} %pad_clamp_fusion) | copy-start | bytes 12292
  11.8 68.8 %copy-start.33 = (f32[1024]{0:T(1024)S(1)}, f32[1024]{0:T(1024)}, u32[]{:S(2)}) copy-start(f32[1024]{0:T(1024)} %param.17) | copy-start | bytes 12292
  45.2 7.1 %all-to-all-start = ((bf16[16,4,128]{2,0,1:T(8,128)(2,1)}), bf16[16,4,128]{2,0,1:T(8,128)(2,1)S(1)}, u32[]{:S(2)}, u32[]{:S(2)}) async-start(bf16[16,4,128]{2,0,1:T(8,128)(2,1)} %bitcast.121), calls=%async_computation | async-start | bytes 32768 | tf_op jit(solution)/shard_map/all_to_all | solution.py:78
  48.5 35.3 %copy-start.28 = (s32[1024]{0:T(1024)}, s32[1024]{0:T(1024)S(1)}, u32[]{:S(2)}) copy-start(s32[1024]{0:T(1024)S(1)} %pad_clamp_fusion.1) | copy-start | bytes 12292
  73.8 10.0 %copy-start.38 = (f32[128]{0:T(128)}, f32[128]{0:T(128)S(1)}, u32[]{:S(2)}) copy-start(f32[128]{0:T(128)S(1)} %psum.70) | copy-start | bytes 1540
  73.8 10.0 %copy-start.15 = (f32[128]{0:T(128)}, f32[128]{0:T(128)S(1)}, u32[]{:S(2)}) copy-start(f32[128]{0:T(128)S(1)} %add_sqrt_fusion.4) | copy-start | bytes 1540
  75.6 9.4 %collective-permute-start.4 = (bf16[128,128]{0,1:T(8,128)(2,1)S(1)}, bf16[128,128]{0,1:T(8,128)(2,1)S(1)}, u32[]{:S(2)}, u32[]{:S(2)}) collective-permute-start(bf16[128,128]{0,1:T(8,128)(2,1)S(1)} %select_bitcast_fusion.4), channel_id=1, source_target_pairs={{0,4},{4,8},{8,12},{12,16},{16,20},{20,24},{24,28},{28,0},{1,5},{5... | collective-permute-start | bytes 98312 | tf_op jit(solution)/shard_map/ppermute | solution.py:34
  75.8 9.3 %copy-start.3 = (bf16[128,128]{1,0:T(8,128)(2,1)S(1)}, bf16[128,128]{1,0:T(8,128)(2,1)}, u32[]{:S(2)}) copy-start(bf16[128,128]{1,0:T(8,128)(2,1)} %param.23) | copy-start | bytes 98308
  75.8 9.6 %copy-start.6 = (bf16[128,128]{1,0:T(8,128)(2,1)S(1)}, bf16[128,128]{1,0:T(8,128)(2,1)}, u32[]{:S(2)}) copy-start(bf16[128,128]{1,0:T(8,128)(2,1)} %param.22) | copy-start | bytes 98308
  75.8 9.5 %collective-permute-start.3 = (bf16[128,128]{0,1:T(8,128)(2,1)S(1)}, bf16[128,128]{0,1:T(8,128)(2,1)}, u32[]{:S(2)}, u32[]{:S(2)}) collective-permute-start(bf16[128,128]{0,1:T(8,128)(2,1)S(1)} %select_bitcast_fusion.5), channel_id=1, source_target_pairs={{4,0},{8,4},{12,8},{16,12},{20,16},{24,20},{28,24},{0,28},{5,1},{9... | collective-permute-start | bytes 98312 | tf_op jit(solution)/shard_map/ppermute | solution.py:37
  88.0 46.7 %copy-start.12 = (f32[1024]{0:T(1024)S(1)}, f32[1024]{0:T(1024)}, u32[]{:S(2)}) copy-start(f32[1024]{0:T(1024)} %param.19) | copy-start | bytes 12292
  89.8 3.2 collective-permute-start.5
  93.0 3.2 collective-permute-start.6
  96.1 3.2 collective-permute-start.7
  130.7 7.9 %copy-start.16 = (f32[128]{0:T(128)S(1)}, f32[128]{0:T(128)}, u32[]{:S(2)}) copy-start(f32[128]{0:T(128)} %copy-done.15) | copy-start | bytes 1540
  131.5 7.1 %all-to-all-start.1 = ((bf16[16,4,128]{2,0,1:T(8,128)(2,1)}), bf16[16,4,128]{2,0,1:T(8,128)(2,1)S(1)}, u32[]{:S(2)}, u32[]{:S(2)}) async-start(bf16[16,4,128]{2,0,1:T(8,128)(2,1)} %bitcast.120), calls=%async_computation.1 | async-start | bytes 32768 | tf_op jit(solution)/shard_map/all_to_all | solution.py:78
  139.9 36.8 %copy-start.2 = (f32[128,1024]{1,0:T(8,128)}, f32[128,1024]{1,0:T(8,128)S(1)}, u32[]{:S(2)}) copy-start(f32[128,1024]{1,0:T(8,128)S(1)} %get-tuple-element.22) | copy-start | bytes 1572868
  159.3 19.3 %copy-start.23 = (f32[128]{0:T(128)}, f32[128]{0:T(128)S(1)}, u32[]{:S(2)}) copy-start(f32[128]{0:T(128)S(1)} %psum.71) | copy-start | bytes 1540
  176.7 1.9 copy-start.36
  184.3 10.0 %collective-permute-start.9 = (bf16[128,128]{0,1:T(8,128)(2,1)S(1)}, bf16[128,128]{0,1:T(8,128)(2,1)S(1)}, u32[]{:S(2)}, u32[]{:S(2)}) collective-permute-start(bf16[128,128]{0,1:T(8,128)(2,1)S(1)} %select_bitcast_fusion.2), channel_id=1, source_target_pairs={{0,4},{4,8},{8,12},{12,16},{16,20},{20,24},{24,28},{28,0},{1,5},{5... | collective-permute-start | bytes 98312 | tf_op jit(solution)/shard_map/ppermute | solution.py:34
  186.4 8.3 %collective-permute-start.8 = (bf16[128,128]{0,1:T(8,128)(2,1)S(1)}, bf16[128,128]{0,1:T(8,128)(2,1)}, u32[]{:S(2)}, u32[]{:S(2)}) collective-permute-start(bf16[128,128]{0,1:T(8,128)(2,1)S(1)} %select_bitcast_fusion.3), channel_id=1, source_target_pairs={{4,0},{8,4},{12,8},{16,12},{20,16},{24,20},{28,24},{0,28},{5,1},{9... | collective-permute-start | bytes 98312 | tf_op jit(solution)/shard_map/ppermute | solution.py:37
  189.1 5.3 %copy-start.4 = (bf16[128,128]{1,0:T(8,128)(2,1)S(1)}, bf16[128,128]{1,0:T(8,128)(2,1)}, u32[]{:S(2)}) copy-start(bf16[128,128]{1,0:T(8,128)(2,1)} %param.23) | copy-start | bytes 98308
  189.1 5.6 %copy-start.7 = (bf16[128,128]{1,0:T(8,128)(2,1)S(1)}, bf16[128,128]{1,0:T(8,128)(2,1)}, u32[]{:S(2)}) copy-start(bf16[128,128]{1,0:T(8,128)(2,1)} %param.22) | copy-start | bytes 98308
  198.8 49.7 %copy-start.13 = (f32[1024]{0:T(1024)S(1)}, f32[1024]{0:T(1024)}, u32[]{:S(2)}) copy-start(f32[1024]{0:T(1024)} %param.19) | copy-start | bytes 12292
  203.1 3.2 collective-permute-start.10
  206.3 3.2 collective-permute-start.11
  209.5 3.2 collective-permute-start.12
  244.5 7.9 %copy-start.17 = (f32[128]{0:T(128)S(1)}, f32[128]{0:T(128)}, u32[]{:S(2)}) copy-start(f32[128]{0:T(128)} %copy-done.15) | copy-start | bytes 1540
  245.3 7.1 %all-to-all-start.2 = ((bf16[16,4,128]{2,0,1:T(8,128)(2,1)}), bf16[16,4,128]{2,0,1:T(8,128)(2,1)S(1)}, u32[]{:S(2)}, u32[]{:S(2)}) async-start(bf16[16,4,128]{2,0,1:T(8,128)(2,1)} %bitcast.119), calls=%async_computation.2 | async-start | bytes 32768 | tf_op jit(solution)/shard_map/all_to_all | solution.py:78
  272.5 21.5 %copy-start.29 = (f32[128]{0:T(128)}, f32[128]{0:T(128)S(1)}, u32[]{:S(2)}) copy-start(f32[128]{0:T(128)S(1)} %psum.73) | copy-start | bytes 1540
  292.0 20.3 %copy-start.34 = (f32[128]{0:T(128)}, f32[128]{0:T(128)S(1)}, u32[]{:S(2)}) copy-start(f32[128]{0:T(128)S(1)} %psum.74) | copy-start | bytes 1540
  312.2 0.6 copy-start.40
  312.2 0.6 copy-start.25
  318.7 3.6 copy-start.11
  318.7 3.6 copy-start.22
  318.7 4.8 %copy-start.10 = (bf16[128,128]{1,0:T(8,128)(2,1)S(1)}, bf16[128,128]{1,0:T(8,128)(2,1)}, u32[]{:S(2)}) copy-start(bf16[128,128]{1,0:T(8,128)(2,1)} %gather_fusion.4) | copy-start | bytes 98308
  318.7 4.8 %copy-start.20 = (pred[128]{0:T(512)(128)(4,1)S(1)}, pred[128]{0:T(512)(128)(4,1)}, u32[]{:S(2)}) copy-start(pred[128]{0:T(512)(128)(4,1)} %copy-done.19) | copy-start | bytes 388
  318.7 10.6 %copy-start.5 = (bf16[128,128]{1,0:T(8,128)(2,1)S(1)}, bf16[128,128]{1,0:T(8,128)(2,1)}, u32[]{:S(2)}) copy-start(bf16[128,128]{1,0:T(8,128)(2,1)} %param.23) | copy-start | bytes 98308
  318.7 10.9 %copy-start.8 = (bf16[128,128]{1,0:T(8,128)(2,1)S(1)}, bf16[128,128]{1,0:T(8,128)(2,1)}, u32[]{:S(2)}) copy-start(bf16[128,128]{1,0:T(8,128)(2,1)} %param.22) | copy-start | bytes 98308
  322.3 7.0 %collective-permute-start.14 = (bf16[128,128]{0,1:T(8,128)(2,1)S(1)}, bf16[128,128]{0,1:T(8,128)(2,1)S(1)}, u32[]{:S(2)}, u32[]{:S(2)}) collective-permute-start(bf16[128,128]{0,1:T(8,128)(2,1)S(1)} %select_bitcast_fusion), channel_id=1, source_target_pairs={{0,4},{4,8},{8,12},{12,16},{16,20},{20,24},{24,28},{28,0},{1,5},{5... | collective-permute-start | bytes 98312 | tf_op jit(solution)/shard_map/ppermute | solution.py:34
  323.5 6.0 %collective-permute-start.13 = (bf16[128,128]{0,1:T(8,128)(2,1)S(1)}, bf16[128,128]{0,1:T(8,128)(2,1)}, u32[]{:S(2)}, u32[]{:S(2)}) collective-permute-start(bf16[128,128]{0,1:T(8,128)(2,1)S(1)} %select_bitcast_fusion.1), channel_id=1, source_target_pairs={{4,0},{8,4},{12,8},{16,12},{20,16},{24,20},{28,24},{0,28},{5,1},{9... | collective-permute-start | bytes 98312 | tf_op jit(solution)/shard_map/ppermute | solution.py:37
  333.7 49.5 %copy-start.14 = (f32[1024]{0:T(1024)S(1)}, f32[1024]{0:T(1024)}, u32[]{:S(2)}) copy-start(f32[1024]{0:T(1024)} %param.19) | copy-start | bytes 12292
  338.1 3.2 collective-permute-start.15
  341.3 3.2 collective-permute-start.16
  344.5 3.2 collective-permute-start.17
  379.1 7.9 %copy-start.18 = (f32[128]{0:T(128)S(1)}, f32[128]{0:T(128)}, u32[]{:S(2)}) copy-start(f32[128]{0:T(128)} %copy-done.15) | copy-start | bytes 1540
  380.0 7.1 %all-to-all-start.3 = ((bf16[16,4,128]{2,0,1:T(8,128)(2,1)}), bf16[16,4,128]{2,0,1:T(8,128)(2,1)S(1)}, u32[]{:S(2)}, u32[]{:S(2)}) async-start(bf16[16,4,128]{2,0,1:T(8,128)(2,1)} %bitcast.118), calls=%async_computation.3 | async-start | bytes 32768 | tf_op jit(solution)/shard_map/all_to_all | solution.py:78
  386.0 43.0 %copy-start.26 = (f32[128]{0:T(128)S(1)}, f32[128]{0:T(128)}, u32[]{:S(2)}) copy-start(f32[128]{0:T(128)} %copy-done.25) | copy-start | bytes 1540
  410.6 20.7 %copy-start.24 = (f32[128]{0:T(128)S(1)}, f32[128]{0:T(128)}, u32[]{:S(2)}) copy-start(f32[128]{0:T(128)} %copy-done.23) | copy-start | bytes 1540
  410.6 20.7 %copy-start.37 = (f32[128]{0:T(128)S(1)}, f32[128]{0:T(128)}, u32[]{:S(2)}) copy-start(f32[128]{0:T(128)} %copy-done.36) | copy-start | bytes 1540
  411.9 57.2 %copy-start.30 = (f32[128]{0:T(128)S(1)}, f32[128]{0:T(128)}, u32[]{:S(2)}) copy-start(f32[128]{0:T(128)} %copy-done.29) | copy-start | bytes 1540
  411.9 57.2 %copy-start.35 = (f32[128]{0:T(128)S(1)}, f32[128]{0:T(128)}, u32[]{:S(2)}) copy-start(f32[128]{0:T(128)} %copy-done.34) | copy-start | bytes 1540
  411.9 57.2 %copy-start.39 = (f32[128]{0:T(128)S(1)}, f32[128]{0:T(128)}, u32[]{:S(2)}) copy-start(f32[128]{0:T(128)} %copy-done.38) | copy-start | bytes 1540
  411.9 57.2 %copy-start.41 = (f32[128]{0:T(128)S(1)}, f32[128]{0:T(128)}, u32[]{:S(2)}) copy-start(f32[128]{0:T(128)} %copy-done.40) | copy-start | bytes 1540
